TPU v7x, 768 devices: a whole 4x8x12 slice. The times are simulated.
768 devices in a mesh: row: 16 (over x, z_hi), col: 48 (over y, z_lo, core).
Axes of the slice: x: 4, y: 8, z: 12 (z_hi: 4, z_lo: 3; z = z_hi * 3 + z_lo), core: 2. Of those that a mesh axis runs over, the one named last changes fastest.
Arguments:
- data: float32 [24576, 36864], P('row', 'col'), may hold values from 0.1 to 10
- w_factor: float32 [24576, 128], P(('row', 'col')), may hold values from 0.01 to 1
- h_factor: float32 [36864, 128], P(('col', 'row')), may hold values from 0.01 to 1
Outputs:
- w_final: float32 [24576, 128], P(('row', 'col'))
- h_final: float32 [36864, 128], P(('col', 'row'))
All inputs are finite; a program needn't handle non-finite values.
Results may differ from a plain program's by a relative error of at most 0.0003.
Values sent between devices are 32-bit elements; how exact they have to be, the bound alone decides.
No kernel may reach another device: no remote copies, remote signals or barrier semaphores. Data moves between devices by JAX's collectives and lax.ppermute only.
A program may use at most 32 MiB of HBM per device.

v0:
```python
import functools

import jax
import jax.numpy as jnp
from jax import lax
from jax.experimental import pallas as pl
from jax.experimental.pallas import tpu as pltpu
from jax.sharding import Mesh, PartitionSpec as P

ITERS = 2
X, ZH, Y, ZL, C = 4, 4, 8, 3, 2
COL = ("zl", "y")
H_PAD, W_PAD = 8, 1
PIECE = 256
VMEM, FIRST_VMEM, MOST_VMEM = 48 * 2**20, 51 * 2**20, 60 * 2**20


def split(a):
    high = a.astype(jnp.bfloat16)
    return high, (a - high.astype(jnp.float32)).astype(jnp.bfloat16)


def half_kernel(fetch, read, groups, pad, which_ref, a_ref, b_ref, *refs):
    d_refs, (o_ref, d_all, b_wide, b_pair, sems) = refs[:-5], refs[-5:]
    n, k = b_ref.shape
    rows = o_ref.shape[0] - groups * pad
    which = which_ref[0]
    copies = fetch(which, d_refs, d_all, sems)
    for copy in copies:
        copy.start()
    b = b_ref[...]
    high, low = split(b.T)
    b_wide[...] = jnp.concatenate([high, high, low], axis=0)
    b_pair[...] = jnp.concatenate(split(b), axis=1)
    b_sum = jnp.broadcast_to(jnp.sum(b, axis=0, keepdims=True), (pad, k))
    high, low = split(a_ref[pl.ds(pl.multiple_of(which * rows, rows), rows), :])
    a_wide = jnp.concatenate([high, low, high], axis=1)
    total = jnp.zeros((rows, 2 * k), jnp.float32)
    pieces = [pl.ds(at, PIECE) for at in range(0, n, PIECE)]

    def model_of(cols):
        return jnp.dot(a_wide, b_wide[:, cols], preferred_element_type=jnp.float32)

    later = model_of(pieces[0])
    part = len(pieces) // len(copies)
    for i, cols in enumerate(pieces):
        if i % part == 0:
            copies[i // part].wait()
        model = later
        if i + 1 < len(pieces):
            later = model_of(pieces[i + 1])
        guess = pltpu.reciprocal(model, approx=True)
        high, low = split(read(d_all, cols) * (guess * (2.0 - model * guess)))
        pair = b_pair[cols, :]
        total += jnp.dot(high, pair, preferred_element_type=jnp.float32)
        total += jnp.dot(low, pair, preferred_element_type=jnp.float32)
    numer = total[:, :k] + total[:, k:]
    each = rows // groups
    for g in range(groups):
        start = g * (each + pad)
        o_ref[pl.ds(start, each), :] = numer[g * each : (g + 1) * each]
        o_ref[pl.ds(start + each, pad), :] = b_sum


def half(fetch, read, d, d_shape, a, b, rows, groups, pad, which, limit=VMEM):
    n, k = b.shape
    whole = pl.BlockSpec(memory_space=pltpu.VMEM)
    return pl.pallas_call(
        functools.partial(half_kernel, fetch, read, groups, pad),
        in_specs=[pl.BlockSpec(memory_space=pltpu.SMEM), whole, whole] + [pl.BlockSpec(memory_space=pl.ANY)] * len(d),
        out_specs=whole,
        out_shape=jax.ShapeDtypeStruct((rows + groups * pad, k), jnp.float32),
        scratch_shapes=[
            pltpu.VMEM(d_shape, jnp.float32),
            pltpu.VMEM((3 * k, n), jnp.bfloat16),
            pltpu.VMEM((n, 2 * k), jnp.bfloat16),
            pltpu.SemaphoreType.DMA((len(d),)),
        ],
        compiler_params=pltpu.CompilerParams(vmem_limit_bytes=limit),
        cost_estimate=pl.CostEstimate(flops=12 * rows * n * k, bytes_accessed=4 * rows * n, transcendentals=0),
    )(which, a, b, *d)


def half_h(dt, h_panel, w_panel, limit):
    n, k = h_panel.shape

    def fetch(which, refs, held, sems):
        width = refs[0].shape[1]
        parts = [held.at[:, pl.ds(i * width, width)] for i in range(len(refs))]
        return [pltpu.make_async_copy(ref, part, sems.at[i]) for i, (ref, part) in enumerate(zip(refs, parts))]

    def read(held, cols):
        return held[:, cols]

    first = jnp.zeros((1,), jnp.int32)
    return half(fetch, read, dt, (n, w_panel.shape[0]), h_panel, w_panel, n, X, H_PAD, first, limit).reshape(X, -1, k)


def half_w(d5, w_panel, h_panel, core):
    rows, n = d5.shape[3], d5.shape[4]
    block = ZL * Y * rows

    def fetch(which, refs, held, sems):
        return [pltpu.make_async_copy(refs[0].at[:, :, which], held, sems.at[0])]

    def read(held, cols):
        return jnp.swapaxes(held[:, :, :, cols], 0, 1).reshape(block, -1)

    return half(fetch, read, [d5], (Y, ZL, rows, n), w_panel, h_panel, block, ZL * Y, W_PAD, core)


def update_kernel(copies, parts_ref, w_ref, o_ref, *copies_ref):
    rows = w_ref.shape[0]
    each = rows + W_PAD
    total = parts_ref[pl.ds(0, each), :]
    for g in range(1, copies):
        total += parts_ref[pl.ds(g * each, each), :]
    w = w_ref[...] * total[:rows] / total[rows : rows + 1]
    o_ref[...] = w
    for ref in copies_ref:
        for g in range(copies):
            ref[g] = w


def update(parts, w, last):
    copies = ZL * Y
    whole = pl.BlockSpec(memory_space=pltpu.VMEM)
    shapes = [jax.ShapeDtypeStruct(w.shape, w.dtype)]
    if not last:
        shapes.append(jax.ShapeDtypeStruct((copies,) + w.shape, w.dtype))
    return pl.pallas_call(
        functools.partial(update_kernel, copies),
        in_specs=[whole, whole],
        out_specs=[whole] * len(shapes),
        out_shape=shapes,
        compiler_params=pltpu.CompilerParams(vmem_limit_bytes=VMEM),
    )(parts, w)


def turn_kernel(d_ref, *o_refs):
    n = d_ref.shape[-1]
    for c, o_ref in enumerate(o_refs):
        o_ref[...] = d_ref[:, 0, c].reshape(-1, n).T


def turned(d5):
    rows, n = d5.shape[3], d5.shape[4]
    return pl.pallas_call(
        turn_kernel,
        grid=(ZL,),
        in_specs=[pl.BlockSpec((Y, 1, C, rows, n), lambda i: (0, i, 0, 0, 0))],
        out_specs=[pl.BlockSpec((n, Y * rows), lambda i: (0, i))] * C,
        out_shape=[jax.ShapeDtypeStruct((n, ZL * Y * rows), jnp.float32)] * C,
        compiler_params=pltpu.CompilerParams(vmem_limit_bytes=MOST_VMEM),
        cost_estimate=pl.CostEstimate(flops=0, bytes_accessed=8 * d5.size, transcendentals=0),
    )(d5)


def exchange(chunks, axes):
    return lax.all_to_all(chunks, axes, 0, 0, tiled=True)


def spread(part, axes, n):
    whole = exchange(jnp.broadcast_to(part[None], (n,) + part.shape), axes)
    return whole.reshape((-1,) + part.shape[1:])


def gather_w(copies):
    whole = exchange(copies, COL).reshape(-1, copies.shape[2])
    return lax.all_gather(whole, "c", axis=0, tiled=True)


def on_device(data, w, h):
    (w_rows, k), h_rows = w.shape, h.shape[0]
    d5 = data.reshape(Y, ZL, C, w_rows, data.shape[1])
    core = lax.axis_index("c").astype(jnp.int32).reshape(1)
    w_panel = gather_w(jnp.broadcast_to(w[None], (ZL * Y,) + w.shape))
    dt = turned(d5)
    h_x = lax.all_gather(h, "zh", axis=0, tiled=True)
    h_x, core, other = lax.optimization_barrier((h_x, core, 1 - core))
    h_panel = spread(h_x, "x", X)
    for step in range(ITERS):
        part = half_h(dt, h_panel, w_panel, FIRST_VMEM if step == 0 else VMEM)
        part = jnp.sum(exchange(part, "x"), axis=0)
        part = jnp.sum(lax.all_gather(part, "zh", axis=0), axis=0)
        h_x = h_x * part[: ZH * h_rows] / part[ZH * h_rows]
        h_panel = spread(h_x, "x", X)
        sent = lax.ppermute(half_w(d5, w_panel, h_panel, other), "c", [(0, 1), (1, 0)])
        part = half_w(d5, w_panel, h_panel, core) + sent
        part = exchange(part.reshape(ZL * Y, 1, -1), COL).reshape(-1, k)
        last = step == ITERS - 1
        w, *copies = update(part, w, last)
        if not last:
            w_panel = gather_w(*copies)
    return w, lax.dynamic_slice_in_dim(h_x, lax.axis_index("zh") * h_rows, h_rows, 0)


def solution(mesh):
    fine = Mesh(mesh.devices.reshape(X, ZH, Y, ZL, C), ("x", "zh", "y", "zl", "c"))
    row, col = ("x", "zh"), ("y", "zl", "c")
    in_specs = (P(row, col), P(row + col, None), P(col + row, None))
    out_specs = (P(row + col, None), P(col + row, None))
    return jax.shard_map(on_device, mesh=fine, in_specs=in_specs, out_specs=out_specs, check_vma=False)
```

profile of v0, /device:TPU:8, one launch (start us, length us, event | category | flops | bytes accessed | tf_op | source)
XLA Modules:
  0.0 223.0 jit_solution(17574643991969884451)
XLA Ops:
  0.6 1.5 broadcast_in_dim.8
  2.1 13.0 %all-to-all-start = ((f32[24,32,128]{2,1,0:T(8,128)}), f32[24,32,128]{2,1,0:T(8,128)S(1)}, u32[]{:S(2)}, u32[]{:S(2)}) async-start(f32[24,32,128]{2,1,0:T(8,128)} %broadcast_in_dim.8), calls=%async_computation | async-start | bytes 786432 | tf_op jit(solution)/shard_map/all_to_all | solution.py:160
  15.2 23.8 %all_gather.21 = f32[192,128]{1,0:T(8,128)S(1)} all-gather(f32[48,128]{1,0:T(8,128)} %param.5), channel_id=1, replica_groups=mesh['x'=4,'zh'=4,'y'=8,'zl'=3,'c'=2] {'zh'}, dimensions={0}, use_global_device_ids=true | all-gather | bytes 122880 | tf_op jit(solution)/shard_map/all_gather | solution.py:179
  39.0 0.0 all-to-all-done
  39.0 0.8 broadcast_in_dim.9
  39.8 4.3 %all-to-all-start.1 = ((f32[4,192,128]{2,1,0:T(8,128)}), f32[4,192,128]{2,1,0:T(8,128)S(1)}, u32[]{:S(2)}, u32[]{:S(2)}) async-start(f32[4,192,128]{2,1,0:T(8,128)} %broadcast_in_dim.9), calls=%async_computation.1 | async-start | bytes 786432 | tf_op jit(solution)/shard_map/all_to_all | solution.py:160
  44.1 5.7 %shard_map.50 = (f32[768,768]{1,0:T(8,128)}, f32[768,768]{1,0:T(8,128)}) custom-call(f32[8,3,2,32,768]{4,3,2,1,0:T(8,128)} %bitcast.29), custom_call_target="tpu_custom_call" | custom-call | bytes 9437184 | tf_op jit(solution)/shard_map/pallas_call | solution.py:148
  49.8 2.4 %all_gather.22.b_ref.a_ref = f32[1536,128]{1,0:T(8,128)S(1)} all-gather(f32[768,128]{1,0:T(8,128)S(1)} %bitcast.37), channel_id=1, replica_groups=mesh['x'=4,'zh'=4,'y'=8,'zl'=3,'c'=2] {'c'}, dimensions={0}, use_global_device_ids=true | all-gather | bytes 1179648 | tf_op jit(solution)/shard_map/all_gather | solution.py:170
  52.1 0.0 all-to-all-done.1
  52.1 4.6 %shard_map.51 = f32[800,128]{1,0:T(8,128)S(1)} custom-call(s32[1]{0:T(128)} %constant.3.clone.1.which_ref, f32[768,128]{1,0:T(8,128)S(1)} %bitcast.28, f32[1536,128]{1,0:T(8,128)S(1)} %all_gather.22.b_ref.a_ref, f32[768,768]{1,0:T(8,128)} %get-tuple-element.11.refs_0_, f32[768,768]{1,0:T(8,128)} %get-tuple-element.12.refs_1_), custom_call_target="tpu_custom_call" | custom-call | flops 1811939328 | bytes 4718592 | tf_op jit(solution)/shard_map/pallas_call | solution.py:68
  56.7 13.1 %all_to_all.45 = f32[4,200,128]{2,1,0:T(8,128)S(1)} all-to-all(f32[4,200,128]{2,1,0:T(8,128)S(1)} %bitcast.27), channel_id=1, replica_groups=mesh['x'=4,'zh'=4,'y'=8,'zl'=3,'c'=2] {'x'}, dimensions={0} | all-to-all | bytes 819200 | tf_op jit(solution)/shard_map/all_to_all | solution.py:160
  69.9 20.2 %all-gather = f32[800,128]{1,0:T(8,128)S(1)} all-gather(f32[200,128]{1,0:T(8,128)S(1)} %reduce_sum.36), channel_id=2, replica_groups=mesh['x'=4,'zh'=4,'y'=8,'zl'=3,'c'=2] {'zh'}, dimensions={0}, use_global_device_ids=true | all-gather | bytes 512000 | tf_op jit(solution)/shard_map/all_gather | solution.py:185
  90.2 9.8 %all_to_all.46 = f32[4,192,128]{2,1,0:T(8,128)S(1)} all-to-all(f32[4,192,128]{2,1,0:T(8,128)S(1)} %broadcast_in_dim.10), channel_id=1, replica_groups=mesh['x'=4,'zh'=4,'y'=8,'zl'=3,'c'=2] {'x'}, dimensions={0} | all-to-all | bytes 786432 | tf_op jit(solution)/shard_map/all_to_all | solution.py:160
  100.0 2.9 %shard_map.53 = f32[792,128]{1,0:T(8,128)S(1)} custom-call(s32[1]{0:T(128)S(6)} %sub.3.which_ref, f32[1536,128]{1,0:T(8,128)S(1)} %all_gather.22.b_ref.a_ref, f32[768,128]{1,0:T(8,128)S(1)} %bitcast.19, f32[8,3,2,32,768]{4,3,2,1,0:T(8,128)} %bitcast.30), custom_call_target="tpu_custom_call" | custom-call | flops 905969664 | bytes 2359296 | tf_op jit(solution)/shard_map/pallas_call | solution.py:68
  102.9 0.0 copy-start
  102.9 1.9 collective-permute-start
  104.8 2.9 %shard_map.52 = f32[792,128]{1,0:T(8,128)S(1)} custom-call(s32[1]{0:T(128)} %bitcast.which_ref, f32[1536,128]{1,0:T(8,128)S(1)} %all_gather.22.b_ref.a_ref, f32[768,128]{1,0:T(8,128)S(1)} %bitcast.20, f32[8,3,2,32,768]{4,3,2,1,0:T(8,128)} %bitcast.31), custom_call_target="tpu_custom_call" | custom-call | flops 905969664 | bytes 2359296 | tf_op jit(solution)/shard_map/pallas_call | solution.py:68
  107.7 0.0 copy-start.1
  107.7 0.0 collective-permute-done
  107.8 21.1 %all_to_all.47 = f32[24,1,4224]{2,1,0:T(1,128)S(1)} all-to-all(f32[24,1,4224]{2,1,0:T(1,128)S(1)} %bitcast.36), channel_id=1, replica_groups=mesh['x'=4,'zh'=4,'y'=8,'zl'=3,'c'=2] {'zl','y'}, dimensions={0} | all-to-all | bytes 811008 | tf_op jit(solution)/shard_map/all_to_all | solution.py:160
  128.8 0.0 copy-done
  128.8 0.1 shard_map.54
  128.9 18.5 %all_to_all.48 = f32[24,32,128]{2,1,0:T(8,128)S(1)} all-to-all(f32[24,32,128]{2,1,0:T(8,128)S(1)} %get-tuple-element.14), channel_id=1, replica_groups=mesh['x'=4,'zh'=4,'y'=8,'zl'=3,'c'=2] {'zl','y'}, dimensions={0} | all-to-all | bytes 786432 | tf_op jit(solution)/shard_map/all_to_all | solution.py:160
  147.4 2.4 %all_gather.25.b_ref.a_ref = f32[1536,128]{1,0:T(8,128)S(1)} all-gather(f32[768,128]{1,0:T(8,128)S(1)} %bitcast.38), channel_id=1, replica_groups=mesh['x'=4,'zh'=4,'y'=8,'zl'=3,'c'=2] {'c'}, dimensions={0}, use_global_device_ids=true | all-gather | bytes 1179648 | tf_op jit(solution)/shard_map/all_gather | solution.py:170
  149.8 0.0 copy-done.1
  149.8 3.5 %shard_map.55 = f32[800,128]{1,0:T(8,128)S(1)} custom-call(s32[1]{0:T(128)} %constant.3.clone.1.which_ref, f32[768,128]{1,0:T(8,128)S(1)} %bitcast.21, f32[1536,128]{1,0:T(8,128)S(1)} %all_gather.25.b_ref.a_ref, f32[768,768]{1,0:T(8,128)S(1)} %copy-done.1, f32[768,768]{1,0:T(8,128)} %get-tuple-element.12.refs_1_), custom_call_target="tpu_custom_call" | custom-call | flops 1811939328 | bytes 4718592 | tf_op jit(solution)/shard_map/pallas_call | solution.py:68
  153.3 11.2 %all_to_all.49 = f32[4,200,128]{2,1,0:T(8,128)S(1)} all-to-all(f32[4,200,128]{2,1,0:T(8,128)S(1)} %bitcast.26), channel_id=1, replica_groups=mesh['x'=4,'zh'=4,'y'=8,'zl'=3,'c'=2] {'x'}, dimensions={0} | all-to-all | bytes 819200 | tf_op jit(solution)/shard_map/all_to_all | solution.py:160
  164.5 19.7 %all-gather.1 = f32[800,128]{1,0:T(8,128)S(1)} all-gather(f32[200,128]{1,0:T(8,128)S(1)} %reduce_sum.38), channel_id=3, replica_groups=mesh['x'=4,'zh'=4,'y'=8,'zl'=3,'c'=2] {'zh'}, dimensions={0}, use_global_device_ids=true | all-gather | bytes 512000 | tf_op jit(solution)/shard_map/all_gather | solution.py:185
  184.3 10.2 %all_to_all.50 = f32[4,192,128]{2,1,0:T(8,128)S(1)} all-to-all(f32[4,192,128]{2,1,0:T(8,128)S(1)} %broadcast_in_dim.11), channel_id=1, replica_groups=mesh['x'=4,'zh'=4,'y'=8,'zl'=3,'c'=2] {'x'}, dimensions={0} | all-to-all | bytes 786432 | tf_op jit(solution)/shard_map/all_to_all | solution.py:160
  194.5 2.9 %shard_map.57 = f32[792,128]{1,0:T(8,128)S(1)} custom-call(s32[1]{0:T(128)S(6)} %sub.3.which_ref, f32[1536,128]{1,0:T(8,128)S(1)} %all_gather.25.b_ref.a_ref, f32[768,128]{1,0:T(8,128)S(1)} %bitcast.22, f32[8,3,2,32,768]{4,3,2,1,0:T(8,128)} %bitcast.32), custom_call_target="tpu_custom_call" | custom-call | flops 905969664 | bytes 2359296 | tf_op jit(solution)/shard_map/pallas_call | solution.py:68
  197.4 1.9 collective-permute-start.1
  199.4 2.9 %shard_map.56 = f32[792,128]{1,0:T(8,128)S(1)} custom-call(s32[1]{0:T(128)} %bitcast.which_ref, f32[1536,128]{1,0:T(8,128)S(1)} %all_gather.25.b_ref.a_ref, f32[768,128]{1,0:T(8,128)S(1)} %bitcast.23, f32[8,3,2,32,768]{4,3,2,1,0:T(8,128)} %bitcast.33), custom_call_target="tpu_custom_call" | custom-call | flops 905969664 | bytes 2359296 | tf_op jit(solution)/shard_map/pallas_call | solution.py:68
  202.3 0.0 collective-permute-done.1
  202.3 0.8 add.10
  203.1 6.0 %all-to-all-start.8 = ((f32[24,1,4224]{2,1,0:T(1,128)}), f32[24,1,4224]{2,1,0:T(1,128)S(1)}, u32[]{:S(2)}, u32[]{:S(2)}) async-start(f32[24,1,4224]{2,1,0:T(1,128)} %bitcast.15), calls=%async_computation.8 | async-start | bytes 811008 | tf_op jit(solution)/shard_map/all_to_all | solution.py:160
  209.1 0.6 constant_dynamic-slice_fusion
  209.8 12.6 %all-to-all-done.8 = f32[24,1,4224]{2,1,0:T(1,128)S(1)} async-done(((f32[24,1,4224]{2,1,0:T(1,128)}), f32[24,1,4224]{2,1,0:T(1,128)S(1)}, u32[]{:S(2)}, u32[]{:S(2)}) %all-to-all-start.8) | async-done | bytes 405536 | tf_op jit(solution)/shard_map/all_to_all | solution.py:160
  222.4 0.6 shard_map.58
  (11 shorter events, 0.2 us)
Async XLA Ops:
  2.1 36.9 %all-to-all-start = ((f32[24,32,128]{2,1,0:T(8,128)}), f32[24,32,128]{2,1,0:T(8,128)S(1)}, u32[]{:S(2)}, u32[]{:S(2)}) async-start(f32[24,32,128]{2,1,0:T(8,128)} %broadcast_in_dim.8), calls=%async_computation | async-start | bytes 786432 | tf_op jit(solution)/shard_map/all_to_all | solution.py:160
  39.8 12.4 %all-to-all-start.1 = ((f32[4,192,128]{2,1,0:T(8,128)}), f32[4,192,128]{2,1,0:T(8,128)S(1)}, u32[]{:S(2)}, u32[]{:S(2)}) async-start(f32[4,192,128]{2,1,0:T(8,128)} %broadcast_in_dim.9), calls=%async_computation.1 | async-start | bytes 786432 | tf_op jit(solution)/shard_map/all_to_all | solution.py:160
  102.9 26.0 %copy-start = (f32[32,128]{1,0:T(8,128)S(1)}, f32[32,128]{1,0:T(8,128)}, u32[]{:S(2)}) copy-start(f32[32,128]{1,0:T(8,128)} %w_ref.1) | copy-start | bytes 49156
  102.9 4.8 %collective-permute-start = (f32[792,128]{1,0:T(8,128)S(1)}, f32[792,128]{1,0:T(8,128)S(1)}, u32[]{:S(2)}, u32[]{:S(2)}) collective-permute-start(f32[792,128]{1,0:T(8,128)S(1)} %shard_map.53), channel_id=1, source_target_pairs={{0,1},{1,0},{2,3},{3,2},{4,5},{5,4},{6,7},{7,6},{8,9},{9,8},{10,11... | collective-permute-start | bytes 1216520 | tf_op jit(solution)/shard_map/ppermute | solution.py:188
  107.7 42.1 %copy-start.1 = (f32[768,768]{1,0:T(8,128)S(1)}, f32[768,768]{1,0:T(8,128)}, u32[]{:S(2)}) copy-start(f32[768,768]{1,0:T(8,128)} %get-tuple-element.11.refs_0_) | copy-start | bytes 7077892
  197.4 4.8 %collective-permute-start.1 = (f32[792,128]{1,0:T(8,128)S(1)}, f32[792,128]{1,0:T(8,128)S(1)}, u32[]{:S(2)}, u32[]{:S(2)}) collective-permute-start(f32[792,128]{1,0:T(8,128)S(1)} %shard_map.57), channel_id=1, source_target_pairs={{0,1},{1,0},{2,3},{3,2},{4,5},{5,4},{6,7},{7,6},{8,9},{9,8},{10,11... | collective-permute-start | bytes 1216520 | tf_op jit(solution)/shard_map/ppermute | solution.py:188
  203.1 19.3 %all-to-all-start.8 = ((f32[24,1,4224]{2,1,0:T(1,128)}), f32[24,1,4224]{2,1,0:T(1,128)S(1)}, u32[]{:S(2)}, u32[]{:S(2)}) async-start(f32[24,1,4224]{2,1,0:T(1,128)} %bitcast.15), calls=%async_computation.8 | async-start | bytes 811008 | tf_op jit(solution)/shard_map/all_to_all | solution.py:160
where the time goes:
time: 224 us; the launch traced here: 223 us
  blocking collectives  152 us (68%)
  starting transfers between devices  27.2 us (12%)
  Pallas kernels  26.1 us (12%)
  waiting for transfers between devices  12.6 us (6%)
  local copies, waits for them, and re-layouts  2.97 us (1%)
    all_to_all x6, blocking collectives, exchange(): return lax.all_to_all(chunks, axes, 0, 0, tiled=True)  83.9 us
    all_gather x2, blocking collectives, on_device(): part = jnp.sum(lax.all_gather(part, 'zh', axis=0), axis=0)  39.9 us
    all_gather x1, blocking collectives, on_device(): h_x = lax.all_gather(h, 'zh', axis=0, tiled=True)  23.8 us
    all_to_all x3, starting transfers between devices, exchange(): return lax.all_to_all(chunks, axes, 0, 0, tiled=True)  23.4 us
    pallas_call x6, Pallas kernels, half(): pl.pallas_call(functools.partial(half_kernel, fetch, read, groups, pad),...  19.7 us
    all_to_all x3, waiting for transfers between devices, exchange(): return lax.all_to_all(chunks, axes, 0, 0, tiled=True)  12.6 us
    pallas_call x1, Pallas kernels, turned(): pl.pallas_call(turn_kernel, grid=(ZL,), in_specs=[pl.BlockSpec((Y, 1, C,...  5.7 us
    all_gather x2, blocking collectives, gather_w(): return lax.all_gather(whole, 'c', axis=0, tiled=True)  4.71 us
  transfers between devices with their start and end apart: 5, of which 1 were waited for; matrix products, arithmetic and copies ran while one was open for 0% of the time, Pallas kernels for 5%

commit v1 on v0

--- a/solution.py
+++ b/solution.py
@@ -12,7 +12,7 @@
 COL = ("zl", "y")
 H_PAD, W_PAD = 8, 1
 PIECE = 256
-VMEM, FIRST_VMEM, MOST_VMEM = 48 * 2**20, 51 * 2**20, 60 * 2**20
+VMEM, NEXT_VMEM, FIRST_VMEM, MOST_VMEM = 48 * 2**20, 36 * 2**20, 51 * 2**20, 60 * 2**20
 
 
 def split(a):
@@ -180,7 +180,7 @@
     h_x, core, other = lax.optimization_barrier((h_x, core, 1 - core))
     h_panel = spread(h_x, "x", X)
     for step in range(ITERS):
-        part = half_h(dt, h_panel, w_panel, FIRST_VMEM if step == 0 else VMEM)
+        part = half_h(dt, h_panel, w_panel, FIRST_VMEM if step == 0 else NEXT_VMEM)
         part = jnp.sum(exchange(part, "x"), axis=0)
         part = jnp.sum(lax.all_gather(part, "zh", axis=0), axis=0)
         h_x = h_x * part[: ZH * h_rows] / part[ZH * h_rows]

time: 224 us -> 224 us (level)
  no operation moved by 1% of the time
where the time goes in v1:
time: 224 us; the launch traced here: 223 us
  blocking collectives  151 us (67%)
  starting transfers between devices  28.2 us (13%)
  Pallas kernels  26.6 us (12%)
  waiting for transfers between devices  12.6 us (6%)
  local copies, waits for them, and re-layouts  2.98 us (1%)
    all_to_all x6, blocking collectives, exchange(): return lax.all_to_all(chunks, axes, 0, 0, tiled=True)  84.7 us
    all_gather x2, blocking collectives, on_device(): part = jnp.sum(lax.all_gather(part, 'zh', axis=0), axis=0)  37.8 us
    all_to_all x3, starting transfers between devices, exchange(): return lax.all_to_all(chunks, axes, 0, 0, tiled=True)  24.3 us
    all_gather x1, blocking collectives, on_device(): h_x = lax.all_gather(h, 'zh', axis=0, tiled=True)  23.8 us
    pallas_call x6, Pallas kernels, half(): pl.pallas_call(functools.partial(half_kernel, fetch, read, groups, pad),...  20.1 us
    all_to_all x3, waiting for transfers between devices, exchange(): return lax.all_to_all(chunks, axes, 0, 0, tiled=True)  12.6 us
    pallas_call x1, Pallas kernels, turned(): pl.pallas_call(turn_kernel, grid=(ZL,), in_specs=[pl.BlockSpec((Y, 1, C,...  5.7 us
    all_gather x2, blocking collectives, gather_w(): return lax.all_gather(whole, 'c', axis=0, tiled=True)  4.71 us
  transfers between devices with their start and end apart: 5, of which 1 were waited for; matrix products, arithmetic and copies ran while one was open for 0% of the time, Pallas kernels for 5%

profile of v1, /device:TPU:8, one launch (start us, length us, event | category | flops | bytes accessed | tf_op | source)
XLA Modules:
  0.0 223.2 jit_solution(14003776211357771442)
XLA Ops:
  0.6 1.5 broadcast_in_dim.8
  2.1 13.0 %all-to-all-start = ((f32[24,32,128]{2,1,0:T(8,128)}), f32[24,32,128]{2,1,0:T(8,128)S(1)}, u32[]{:S(2)}, u32[]{:S(2)}) async-start(f32[24,32,128]{2,1,0:T(8,128)} %broadcast_in_dim.8), calls=%async_computation | async-start | bytes 786432 | tf_op jit(solution)/shard_map/all_to_all | solution.py:160
  15.2 23.8 %all_gather.21 = f32[192,128]{1,0:T(8,128)S(1)} all-gather(f32[48,128]{1,0:T(8,128)} %param.5), channel_id=1, replica_groups=mesh['x'=4,'zh'=4,'y'=8,'zl'=3,'c'=2] {'zh'}, dimensions={0}, use_global_device_ids=true | all-gather | bytes 122880 | tf_op jit(solution)/shard_map/all_gather | solution.py:179
  39.0 0.0 all-to-all-done
  39.0 0.8 broadcast_in_dim.9
  39.8 4.3 %all-to-all-start.1 = ((f32[4,192,128]{2,1,0:T(8,128)}), f32[4,192,128]{2,1,0:T(8,128)S(1)}, u32[]{:S(2)}, u32[]{:S(2)}) async-start(f32[4,192,128]{2,1,0:T(8,128)} %broadcast_in_dim.9), calls=%async_computation.1 | async-start | bytes 786432 | tf_op jit(solution)/shard_map/all_to_all | solution.py:160
  44.1 5.7 %shard_map.50 = (f32[768,768]{1,0:T(8,128)}, f32[768,768]{1,0:T(8,128)}) custom-call(f32[8,3,2,32,768]{4,3,2,1,0:T(8,128)} %bitcast.29), custom_call_target="tpu_custom_call" | custom-call | bytes 9437184 | tf_op jit(solution)/shard_map/pallas_call | solution.py:148
  49.8 2.4 %all_gather.22.b_ref.a_ref = f32[1536,128]{1,0:T(8,128)S(1)} all-gather(f32[768,128]{1,0:T(8,128)S(1)} %bitcast.37), channel_id=1, replica_groups=mesh['x'=4,'zh'=4,'y'=8,'zl'=3,'c'=2] {'c'}, dimensions={0}, use_global_device_ids=true | all-gather | bytes 1179648 | tf_op jit(solution)/shard_map/all_gather | solution.py:170
  52.1 0.0 all-to-all-done.1
  52.1 4.6 %shard_map.51 = f32[800,128]{1,0:T(8,128)S(1)} custom-call(s32[1]{0:T(128)} %constant.3.clone.1.which_ref, f32[768,128]{1,0:T(8,128)S(1)} %bitcast.28, f32[1536,128]{1,0:T(8,128)S(1)} %all_gather.22.b_ref.a_ref, f32[768,768]{1,0:T(8,128)} %get-tuple-element.11.refs_0_, f32[768,768]{1,0:T(8,128)} %get-tuple-element.12.refs_1_), custom_call_target="tpu_custom_call" | custom-call | flops 1811939328 | bytes 4718592 | tf_op jit(solution)/shard_map/pallas_call | solution.py:68
  56.7 13.1 %all_to_all.45 = f32[4,200,128]{2,1,0:T(8,128)S(1)} all-to-all(f32[4,200,128]{2,1,0:T(8,128)S(1)} %bitcast.27), channel_id=1, replica_groups=mesh['x'=4,'zh'=4,'y'=8,'zl'=3,'c'=2] {'x'}, dimensions={0} | all-to-all | bytes 819200 | tf_op jit(solution)/shard_map/all_to_all | solution.py:160
  69.9 19.0 %all-gather = f32[800,128]{1,0:T(8,128)S(1)} all-gather(f32[200,128]{1,0:T(8,128)S(1)} %reduce_sum.36), channel_id=2, replica_groups=mesh['x'=4,'zh'=4,'y'=8,'zl'=3,'c'=2] {'zh'}, dimensions={0}, use_global_device_ids=true | all-gather | bytes 512000 | tf_op jit(solution)/shard_map/all_gather | solution.py:185
  89.1 10.7 %all_to_all.46 = f32[4,192,128]{2,1,0:T(8,128)S(1)} all-to-all(f32[4,192,128]{2,1,0:T(8,128)S(1)} %broadcast_in_dim.10), channel_id=1, replica_groups=mesh['x'=4,'zh'=4,'y'=8,'zl'=3,'c'=2] {'x'}, dimensions={0} | all-to-all | bytes 786432 | tf_op jit(solution)/shard_map/all_to_all | solution.py:160
  99.7 2.9 %shard_map.53 = f32[792,128]{1,0:T(8,128)S(1)} custom-call(s32[1]{0:T(128)S(6)} %sub.3.which_ref, f32[1536,128]{1,0:T(8,128)S(1)} %all_gather.22.b_ref.a_ref, f32[768,128]{1,0:T(8,128)S(1)} %bitcast.19, f32[8,3,2,32,768]{4,3,2,1,0:T(8,128)} %bitcast.30), custom_call_target="tpu_custom_call" | custom-call | flops 905969664 | bytes 2359296 | tf_op jit(solution)/shard_map/pallas_call | solution.py:68
  102.6 0.0 copy-start
  102.6 1.9 collective-permute-start
  104.6 0.0 copy-start.2
  104.6 3.0 %shard_map.52 = f32[792,128]{1,0:T(8,128)S(1)} custom-call(s32[1]{0:T(128)} %bitcast.which_ref, f32[1536,128]{1,0:T(8,128)S(1)} %all_gather.22.b_ref.a_ref, f32[768,128]{1,0:T(8,128)S(1)} %bitcast.20, f32[8,3,2,32,768]{4,3,2,1,0:T(8,128)} %bitcast.31), custom_call_target="tpu_custom_call" | custom-call | flops 905969664 | bytes 2359296 | tf_op jit(solution)/shard_map/pallas_call | solution.py:68
  107.6 0.0 copy-start.1
  107.7 0.0 collective-permute-done
  107.7 21.1 %all_to_all.47 = f32[24,1,4224]{2,1,0:T(1,128)S(1)} all-to-all(f32[24,1,4224]{2,1,0:T(1,128)S(1)} %bitcast.36), channel_id=1, replica_groups=mesh['x'=4,'zh'=4,'y'=8,'zl'=3,'c'=2] {'zl','y'}, dimensions={0} | all-to-all | bytes 811008 | tf_op jit(solution)/shard_map/all_to_all | solution.py:160
  128.8 0.0 copy-done
  128.8 0.1 shard_map.54
  128.9 18.5 %all_to_all.48 = f32[24,32,128]{2,1,0:T(8,128)S(1)} all-to-all(f32[24,32,128]{2,1,0:T(8,128)S(1)} %get-tuple-element.14), channel_id=1, replica_groups=mesh['x'=4,'zh'=4,'y'=8,'zl'=3,'c'=2] {'zl','y'}, dimensions={0} | all-to-all | bytes 786432 | tf_op jit(solution)/shard_map/all_to_all | solution.py:160
  147.3 2.4 %all_gather.25.b_ref.a_ref = f32[1536,128]{1,0:T(8,128)S(1)} all-gather(f32[768,128]{1,0:T(8,128)S(1)} %bitcast.38), channel_id=1, replica_groups=mesh['x'=4,'zh'=4,'y'=8,'zl'=3,'c'=2] {'c'}, dimensions={0}, use_global_device_ids=true | all-gather | bytes 1179648 | tf_op jit(solution)/shard_map/all_gather | solution.py:170
  149.7 0.0 copy-done.2
  149.7 0.0 copy-done.1
  149.7 3.8 %shard_map.55 = f32[800,128]{1,0:T(8,128)S(1)} custom-call(s32[1]{0:T(128)} %constant.3.clone.1.which_ref, f32[768,128]{1,0:T(8,128)S(1)} %bitcast.21, f32[1536,128]{1,0:T(8,128)S(1)} %all_gather.25.b_ref.a_ref, f32[768,768]{1,0:T(8,128)S(1)} %copy-done.1, f32[768,768]{1,0:T(8,128)S(1)} %copy-done.2), custom_call_target="tpu_custom_call" | custom-call | flops 1811939328 | bytes 4718592 | tf_op jit(solution)/shard_map/pallas_call | solution.py:68
  153.5 11.2 %all_to_all.49 = f32[4,200,128]{2,1,0:T(8,128)S(1)} all-to-all(f32[4,200,128]{2,1,0:T(8,128)S(1)} %bitcast.26), channel_id=1, replica_groups=mesh['x'=4,'zh'=4,'y'=8,'zl'=3,'c'=2] {'x'}, dimensions={0} | all-to-all | bytes 819200 | tf_op jit(solution)/shard_map/all_to_all | solution.py:160
  164.7 18.8 %all-gather.1 = f32[800,128]{1,0:T(8,128)S(1)} all-gather(f32[200,128]{1,0:T(8,128)S(1)} %reduce_sum.38), channel_id=3, replica_groups=mesh['x'=4,'zh'=4,'y'=8,'zl'=3,'c'=2] {'zh'}, dimensions={0}, use_global_device_ids=true | all-gather | bytes 512000 | tf_op jit(solution)/shard_map/all_gather | solution.py:185
  183.6 10.2 %all_to_all.50 = f32[4,192,128]{2,1,0:T(8,128)S(1)} all-to-all(f32[4,192,128]{2,1,0:T(8,128)S(1)} %broadcast_in_dim.11), channel_id=1, replica_groups=mesh['x'=4,'zh'=4,'y'=8,'zl'=3,'c'=2] {'x'}, dimensions={0} | all-to-all | bytes 786432 | tf_op jit(solution)/shard_map/all_to_all | solution.py:160
  193.8 2.9 %shard_map.57 = f32[792,128]{1,0:T(8,128)S(1)} custom-call(s32[1]{0:T(128)S(6)} %sub.3.which_ref, f32[1536,128]{1,0:T(8,128)S(1)} %all_gather.25.b_ref.a_ref, f32[768,128]{1,0:T(8,128)S(1)} %bitcast.22, f32[8,3,2,32,768]{4,3,2,1,0:T(8,128)} %bitcast.32), custom_call_target="tpu_custom_call" | custom-call | flops 905969664 | bytes 2359296 | tf_op jit(solution)/shard_map/pallas_call | solution.py:68
  196.7 1.9 collective-permute-start.1
  198.6 2.9 %shard_map.56 = f32[792,128]{1,0:T(8,128)S(1)} custom-call(s32[1]{0:T(128)} %bitcast.which_ref, f32[1536,128]{1,0:T(8,128)S(1)} %all_gather.25.b_ref.a_ref, f32[768,128]{1,0:T(8,128)S(1)} %bitcast.23, f32[8,3,2,32,768]{4,3,2,1,0:T(8,128)} %bitcast.33), custom_call_target="tpu_custom_call" | custom-call | flops 905969664 | bytes 2359296 | tf_op jit(solution)/shard_map/pallas_call | solution.py:68
  201.5 0.0 collective-permute-done.1
  201.5 0.8 add.10
  202.3 7.0 %all-to-all-start.8 = ((f32[24,1,4224]{2,1,0:T(1,128)}), f32[24,1,4224]{2,1,0:T(1,128)S(1)}, u32[]{:S(2)}, u32[]{:S(2)}) async-start(f32[24,1,4224]{2,1,0:T(1,128)} %bitcast.15), calls=%async_computation.8 | async-start | bytes 811008 | tf_op jit(solution)/shard_map/all_to_all | solution.py:160
  209.4 0.6 constant_dynamic-slice_fusion
  210.0 12.6 %all-to-all-done.8 = f32[24,1,4224]{2,1,0:T(1,128)S(1)} async-done(((f32[24,1,4224]{2,1,0:T(1,128)}), f32[24,1,4224]{2,1,0:T(1,128)S(1)}, u32[]{:S(2)}, u32[]{:S(2)}) %all-to-all-start.8) | async-done | bytes 405536 | tf_op jit(solution)/shard_map/all_to_all | solution.py:160
  222.6 0.6 shard_map.58
  (11 shorter events, 0.2 us)
Async XLA Ops:
  2.1 36.9 %all-to-all-start = ((f32[24,32,128]{2,1,0:T(8,128)}), f32[24,32,128]{2,1,0:T(8,128)S(1)}, u32[]{:S(2)}, u32[]{:S(2)}) async-start(f32[24,32,128]{2,1,0:T(8,128)} %broadcast_in_dim.8), calls=%async_computation | async-start | bytes 786432 | tf_op jit(solution)/shard_map/all_to_all | solution.py:160
  39.8 12.3 %all-to-all-start.1 = ((f32[4,192,128]{2,1,0:T(8,128)}), f32[4,192,128]{2,1,0:T(8,128)S(1)}, u32[]{:S(2)}, u32[]{:S(2)}) async-start(f32[4,192,128]{2,1,0:T(8,128)} %broadcast_in_dim.9), calls=%async_computation.1 | async-start | bytes 786432 | tf_op jit(solution)/shard_map/all_to_all | solution.py:160
  102.6 26.1 %copy-start = (f32[32,128]{1,0:T(8,128)S(1)}, f32[32,128]{1,0:T(8,128)}, u32[]{:S(2)}) copy-start(f32[32,128]{1,0:T(8,128)} %w_ref.1) | copy-start | bytes 49156
  102.6 5.0 %collective-permute-start = (f32[792,128]{1,0:T(8,128)S(1)}, f32[792,128]{1,0:T(8,128)S(1)}, u32[]{:S(2)}, u32[]{:S(2)}) collective-permute-start(f32[792,128]{1,0:T(8,128)S(1)} %shard_map.53), channel_id=1, source_target_pairs={{0,1},{1,0},{2,3},{3,2},{4,5},{5,4},{6,7},{7,6},{8,9},{9,8},{10,11... | collective-permute-start | bytes 1216520 | tf_op jit(solution)/shard_map/ppermute | solution.py:188
  104.6 45.1 %copy-start.2 = (f32[768,768]{1,0:T(8,128)S(1)}, f32[768,768]{1,0:T(8,128)}, u32[]{:S(2)}) copy-start(f32[768,768]{1,0:T(8,128)} %get-tuple-element.12.refs_1_) | copy-start | bytes 7077892
  107.6 42.0 %copy-start.1 = (f32[768,768]{1,0:T(8,128)S(1)}, f32[768,768]{1,0:T(8,128)}, u32[]{:S(2)}) copy-start(f32[768,768]{1,0:T(8,128)} %get-tuple-element.11.refs_0_) | copy-start | bytes 7077892
  196.7 4.8 %collective-permute-start.1 = (f32[792,128]{1,0:T(8,128)S(1)}, f32[792,128]{1,0:T(8,128)S(1)}, u32[]{:S(2)}, u32[]{:S(2)}) collective-permute-start(f32[792,128]{1,0:T(8,128)S(1)} %shard_map.57), channel_id=1, source_target_pairs={{0,1},{1,0},{2,3},{3,2},{4,5},{5,4},{6,7},{7,6},{8,9},{9,8},{10,11... | collective-permute-start | bytes 1216520 | tf_op jit(solution)/shard_map/ppermute | solution.py:188
  202.3 20.2 %all-to-all-start.8 = ((f32[24,1,4224]{2,1,0:T(1,128)}), f32[24,1,4224]{2,1,0:T(1,128)S(1)}, u32[]{:S(2)}, u32[]{:S(2)}) async-start(f32[24,1,4224]{2,1,0:T(1,128)} %bitcast.15), calls=%async_computation.8 | async-start | bytes 811008 | tf_op jit(solution)/shard_map/all_to_all | solution.py:160
